TPU v7x, 256 devices: a whole 4x4x8 slice. The times are simulated.
256 devices in a mesh: member: 8 (over x_lo, y), grid: 32 (over x_hi, z, core).
Axes of the slice: x: 4 (x_hi: 2, x_lo: 2; x = x_hi * 2 + x_lo), y: 4, z: 8, core: 2. Of those that a mesh axis runs over, the one named last changes fastest.
Arguments:
- latent: bfloat16 [8, 8192, 1024], P('member', 'grid'), may hold values from -6 to 6
- grid_latent_skip: bfloat16 [8, 16384, 1024], P('member', 'grid'), may hold values from -6 to 6
- initial_member_state: float32 [8, 100, 16384], P('member', None, 'grid'), may hold values from -6 to 6
- target: float32 [100, 16384], P(None, 'grid'), may hold values from -6 to 6
- neighbours: int32 [3, 16384], P(None, 'grid'), may hold values from 0 to 511, as said below
- edge_weight: float32 [3, 16384], P(None, 'grid'), may hold values from 0.2 to 1
- area_weight: float32 [16384], P('grid'), may hold values from 0.3 to 27, as said below
- variable_weight: float32 [100], replicated, may hold values from 0.3 to 3
- output_projection: bfloat16 [100, 1024], replicated, may hold values from -0.1875 to 0.1875
- layer_norm_gain: float32 [1024], replicated, may hold values from 0.1 to 1.9
Outputs:
- fair_crps: float32 [], replicated
- latent_grad: bfloat16 [8, 8192, 1024], P('member', 'grid')
- out_weight_grad: float32 [100, 1024], replicated
- norm_gain_grad: float32 [1024], replicated
Inputs may be any that keep to these rules, and one draw needn't show every extreme that they name: neighbours[k, p] indexes 256 + 2 * 128 rows ordered by latitude: the 128 last mesh rows of the slab below the point's slab, the slab's own 256 rows, then the 128 first rows of the slab above. `area_weight`: positive.
All inputs are finite; a program needn't handle non-finite values.
Results may differ from a plain program's by a relative error of at most 0.0067.
Values may be sent and summed in bfloat16 or wider, within the bound.
No kernel may reach another device: no remote copies, remote signals or barrier semaphores. Data moves between devices by JAX's collectives and lax.ppermute only.
A program may use at most 64 MiB of HBM per device.

v0:
```python
import jax
import jax.numpy as jnp
from jax import lax
from jax.sharding import PartitionSpec as P

SMOOTHING = 0.25
FAIRNESS = 0.95
norm_eps = 1e-05


def with_halo(array, sides, width):
    for axis, dim in sides:
        size, length = (lax.axis_size(axis), array.shape[dim])
        up = [(i, (i + 1) % size) for i in range(size - 1)]
        down = [(j, i) for i, j in up]
        last = lax.slice_in_dim(array, length - width, length, axis=dim)
        initial = lax.slice_in_dim(array, 0, width, axis=dim)
        before = lax.ppermute(last, axis, up)
        after = lax.ppermute(initial, axis, down)
        array = jnp.concatenate([before, array, after], axis=dim)
    return array


def from_behind(block, axis, distance):
    devices = range(lax.axis_size(axis))
    route = [(i - distance, i) for i in devices if i - distance in devices]
    return lax.ppermute(block, axis, route)


def smooth_abs(value):
    return jnp.sqrt(value * value + SMOOTHING * SMOOTHING)


def per_device(
    latent,
    grid_latent_skip,
    initial_member_state,
    target,
    neighbours,
    edge_weight,
    area_weight,
    variable_weight,
    output_projection,
    layer_norm_gain,
):
    mesh_count = latent.shape[1]
    rim = mesh_count // 2
    points = grid_latent_skip.shape[1]
    slots = neighbours.shape[0]
    variables = output_projection.shape[0]
    member_list = lax.axis_size("member")
    extended = with_halo(latent, (("grid", 1),), rim)[0]
    weight_arrays = edge_weight / jnp.sum(edge_weight, axis=0, keepdims=True)
    mixed = grid_latent_skip[0].astype(jnp.float32)
    for slot in range(slots):
        mixed = mixed + weight_arrays[slot][:, None] * jnp.take(
            extended, neighbours[slot], axis=0
        ).astype(jnp.float32)
    centred = mixed - jnp.mean(mixed, axis=1, keepdims=True)
    rscale = lax.rsqrt(jnp.mean(centred * centred, axis=1, keepdims=True) + norm_eps)
    normed = centred * rscale
    scaled = (normed * layer_norm_gain[None, :]).astype(jnp.bfloat16)
    predicted_field = initial_member_state[0] + lax.dot_general(
        output_projection, scaled, (((1,), (1,)), ((), ())), preferred_element_type=jnp.float32
    )
    weight_map = variable_weight[:, None] * area_weight[None, :]
    pair_distance = predicted_field - target
    spread = smooth_abs(pair_distance)
    eps_fair = (1.0 - FAIRNESS) / member_list
    coef_pair = (1.0 - eps_fair) / (member_list * (member_list - 1))
    every_member_set = lax.all_gather(predicted_field[None], "member", axis=0, tiled=True)
    member_difference = predicted_field[None] - every_member_set
    dist = smooth_abs(member_difference)
    pair_total = jnp.sum(dist, axis=0) - SMOOTHING
    pair_slope = jnp.sum(member_difference / dist, axis=0)
    pair_loss = jnp.sum(weight_map * pair_total)
    local_loss = jnp.sum(weight_map * spread) / member_list - 0.5 * coef_pair * pair_loss
    fore_grad = (
        weight_map * (pair_distance / spread / member_list - coef_pair * pair_slope)
    ).astype(jnp.bfloat16)
    wout_part = jnp.dot(fore_grad, scaled, preferred_element_type=jnp.float32)
    scaled_grad = lax.dot_general(
        fore_grad, output_projection, (((0,), (0,)), ((), ())), preferred_element_type=jnp.float32
    )
    gain_part = jnp.sum(scaled_grad * normed, axis=0)
    norm_grad = scaled_grad * layer_norm_gain[None, :]
    mixed_grad = rscale * (
        norm_grad
        - jnp.mean(norm_grad, axis=1, keepdims=True)
        - normed * jnp.mean(norm_grad * normed, axis=1, keepdims=True)
    )
    collect = jnp.zeros((extended.shape[0], extended.shape[1]), jnp.float32)
    for slot in range(slots):
        collect = collect.at[neighbours[slot]].add(weight_arrays[slot][:, None] * mixed_grad)
    from_above = from_behind(collect[:rim].astype(jnp.bfloat16), "grid", -1).astype(jnp.float32)
    from_below = from_behind(collect[rim + mesh_count :].astype(jnp.bfloat16), "grid", 1).astype(
        jnp.float32
    )
    owned = collect[rim : rim + mesh_count] + jnp.concatenate([from_below, from_above], axis=0)
    sums = lax.psum((wout_part, gain_part, local_loss), ("member", "grid"))
    fair_crps = sums[2] / (points * lax.axis_size("grid") * variables)
    return (fair_crps, owned[None].astype(jnp.bfloat16), sums[0], sums[1])


def solution(mesh):
    placed = (
        P("member", "grid", None),
        P("member", "grid", None),
        P("member", None, "grid"),
        P(None, "grid"),
        P(None, "grid"),
        P(None, "grid"),
        P("grid"),
        P(),
        P(),
        P(),
    )
    return jax.shard_map(
        per_device,
        mesh=mesh,
        in_specs=placed,
        out_specs=(P(), P("member", "grid", None), P(), P()),
        check_vma=False,
    )
```

profile of v0, /device:TPU:2, one launch (start us, length us, event | category | flops | bytes accessed | tf_op | source)
XLA Modules:
  0.0 378.3 jit_solution(10001090698908370508)
XLA Ops:
  7.2 0.0 copy-start
  7.2 0.0 all-gather.4.cloned.1.call-start
  7.2 1.1 fusion.24
  8.3 1.8 collective-permute-start
  10.1 1.3 collective-permute-start.1
  11.4 0.8 fusion.26
  12.3 0.7 reduce_sum.90
  13.0 0.7 broadcast_divide_fusion
  13.8 0.0 collective-permute-done
  13.8 1.5 collective-permute-done.1
  15.2 1.1 maximum_bitcast_fusion
  16.3 2.1 gather_fusion.2
  18.4 2.8 gather_fusion.1
  21.2 2.8 gather_fusion
  24.0 2.8 fusion.21
  26.8 0.0 copy-start.6
  26.8 0.3 multiply_reduce_fusion.2
  27.2 0.0 copy-start.4
  27.2 0.3 copy-done.6
  27.5 0.0 copy-start.7
  27.5 0.3 multiply_convert_fusion
  27.8 0.0 copy-done
  27.9 0.3 copy-done.4
  28.1 0.0 copy-start.8
  28.1 0.0 copy-start.9
  28.1 1.1 fusion.11
  29.3 0.0 all-gather.4.cloned.1.call-update
  29.3 0.0 all-reduce.3.cloned.1.call-start
  29.4 0.0 copy-done.7
  29.4 49.7 %all-gather.4.cloned.1.call-done = f32[8,100,512]{2,1,0:T(8,128)} async-done(((f32[1,100,512]{2,1,0:T(8,128)}), f32[8,100,512]{2,1,0:T(8,128)}) %all-gather.4.cloned.1.call-update) | async-done | bytes 1638416 | tf_op jit(solution)/shard_map/all_gather | solution.py:71
  79.0 0.0 copy-start.3
  79.0 0.0 copy-start.5
  79.0 2.5 fusion.10
  81.5 0.0 copy-done.8
  81.5 0.0 copy-done.9
  81.5 0.0 copy-done.3
  81.5 0.0 copy-done.5
  81.6 0.8 fusion.19
  82.4 0.9 multiply_reduce_fusion
  83.3 1.9 subtract_multiply_fusion
  85.2 0.0 copy-start.1
  85.2 7.4 %scatter_custom_fusion = f32[512,1024]{1,0:T(8,128)} fusion(s32[512]{0:T(512)S(1)} %bitcast.51, f32[512,1024]{1,0:T(8,128)} %subtract_multiply_fusion, f32[]{:T(128)} %constant.19.clone.1, f32[512]{0:T(512)S(1)} %bitcast.42), kind=kCustom, calls=%fused_computation.14 | custom fusion | flops 1048576 | bytes 4196356 | tf_op jit(solution)/shard_map/scatter-add | solution.py:94
  92.7 0.0 copy-done.1
  92.7 7.7 %scatter_custom_fusion.1 = f32[512,1024]{1,0:T(8,128)} fusion(f32[512,1024]{1,0:T(8,128)} %scatter_custom_fusion, s32[512]{0:T(512)S(1)} %bitcast.50, f32[512,1024]{1,0:T(8,128)S(1)} %copy-done.1, f32[512]{0:T(512)S(1)} %bitcast.40), kind=kCustom, calls=%fused_computation.12 | custom fusion | flops 1048576 | bytes 4196352 | tf_op jit(solution)/shard_map/scatter-add | solution.py:94
  100.4 7.7 %scatter_custom_fusion.2 = f32[512,1024]{1,0:T(8,128)} fusion(f32[512,1024]{1,0:T(8,128)} %scatter_custom_fusion.1, s32[512]{0:T(512)S(1)} %bitcast.49, f32[512,1024]{1,0:T(8,128)S(1)} %copy-done.1, f32[512]{0:T(512)S(1)} %bitcast.38), kind=kCustom, calls=%fused_computation.10 | custom fusion | flops 1048576 | bytes 4196352 | tf_op jit(solution)/shard_map/scatter-add | solution.py:94
  108.2 1.7 convert.6
  109.9 0.0 copy-start.2
  109.9 0.8 fusion.23
  110.8 2.0 collective-permute-start.2
  112.7 1.3 collective-permute-start.3
  114.0 1.1 fusion.27
  115.1 0.0 all-reduce.3.cloned.1.call-update
  116.4 79.3 %all-reduce = (f32[]{:T(128)}, f32[1024]{0:T(1024)}) all-reduce(f32[]{:T(128)S(6)} %sub.46, f32[1024]{0:T(1024)S(1)} %get-tuple-element.5), channel_id=1, replica_groups=mesh['member'=8,'grid'=32] {'member','grid'}, use_global_device_ids=true, to_apply=%region_6.8 | all-reduce | flops 1025 | bytes 8200 | tf_op jit(solution)/shard_map/psum | solution.py:100
  196.3 0.0 collective-permute-done.2
  196.3 0.0 collective-permute-done.3
  196.3 0.0 copy-done.2
  196.4 2.0 fusion.17
  198.3 170.2 %all-reduce.3.cloned.1.call-done = f32[100,1024]{1,0:T(8,128)} async-done(((f32[100,1024]{1,0:T(8,128)}), f32[100,1024]{1,0:T(8,128)}) %all-reduce.3.cloned.1.call-update) | async-done | bytes 409616 | tf_op jit(solution)/shard_map/psum | solution.py:100
  368.6 1.8 copy.19
  (14 shorter events, 0.1 us)
Async XLA Ops:
  7.2 20.7 %copy-start = (bf16[100,1024]{1,0:T(8,128)(2,1)S(1)}, bf16[100,1024]{1,0:T(8,128)(2,1)}, u32[]{:S(2)}) copy-start(bf16[100,1024]{1,0:T(8,128)(2,1)} %param.20) | copy-start | bytes 614404
  7.2 71.9 %all-gather.4.cloned.1.call-start = ((), (), s32[]{:S(2)}) async-start(), calls=%async_computation.1 | async-start | bytes 1916928 | tf_op jit(solution)/shard_map/all_gather | solution.py:71
  8.3 5.4 %collective-permute-start = (bf16[1,128,1024]{2,1,0:T(8,128)(2,1)S(1)}, bf16[1,128,1024]{2,1,0:T(8,128)(2,1)S(1)}, u32[]{:S(2)}, u32[]{:S(2)}) collective-permute-start(bf16[1,128,1024]{2,1,0:T(8,128)(2,1)S(1)} %get-tuple-element.18), channel_id=1, source_target_pairs={{0,1},{1,2},{2,3},{3,4},{4,5},{5,6},{6,7},{7,8},{8,9},{9,10},{10,1... | collective-permute-start | bytes 786440 | tf_op jit(solution)/shard_map/ppermute | solution.py:18
  10.1 5.1 %collective-permute-start.1 = (bf16[1,128,1024]{2,1,0:T(8,128)(2,1)S(1)}, bf16[1,128,1024]{2,1,0:T(8,128)(2,1)S(1)}, u32[]{:S(2)}, u32[]{:S(2)}) collective-permute-start(bf16[1,128,1024]{2,1,0:T(8,128)(2,1)S(1)} %get-tuple-element.19), channel_id=1, source_target_pairs={{1,0},{2,1},{3,2},{4,3},{5,4},{6,5},{7,6},{8,7},{9,8},{10,9},{11,1... | collective-permute-start | bytes 786440 | tf_op jit(solution)/shard_map/ppermute | solution.py:19
  26.8 0.7 copy-start.6
  27.2 0.9 copy-start.4
  27.5 1.8 copy-start.7
  28.1 53.4 %copy-start.8 = (f32[512]{0:T(512)S(1)}, f32[512]{0:T(512)}, u32[]{:S(2)}) copy-start(f32[512]{0:T(512)} %param.18) | copy-start | bytes 6148
  28.1 53.4 %copy-start.9 = (f32[100]{0:T(128)S(1)}, f32[100]{0:T(128)}, u32[]{:S(2)}) copy-start(f32[100]{0:T(128)} %param.19) | copy-start | bytes 1204
  29.3 339.3 %all-reduce.3.cloned.1.call-start = ((), (), s32[]{:S(2)}) async-start(), calls=%async_computation | async-start | bytes 851968 | tf_op jit(solution)/shard_map/psum | solution.py:100
  79.0 2.5 copy-start.3
  79.0 2.5 copy-start.5
  85.2 7.5 %copy-start.1 = (f32[512,1024]{1,0:T(8,128)S(1)}, f32[512,1024]{1,0:T(8,128)}, u32[]{:S(2)}) copy-start(f32[512,1024]{1,0:T(8,128)} %subtract_multiply_fusion) | copy-start | bytes 6291460
  109.9 86.4 %copy-start.2 = (f32[512,1024]{1,0:T(8,128)S(1)}, f32[512,1024]{1,0:T(8,128)}, u32[]{:S(2)}) copy-start(f32[512,1024]{1,0:T(8,128)} %scatter_custom_fusion.2) | copy-start | bytes 6291460
  110.8 85.6 %collective-permute-start.2 = (bf16[128,1024]{1,0:T(8,128)(2,1)}, bf16[128,1024]{1,0:T(8,128)(2,1)}, u32[]{:S(2)}, u32[]{:S(2)}) collective-permute-start(bf16[128,1024]{1,0:T(8,128)(2,1)} %get-tuple-element.16), channel_id=1, source_target_pairs={{0,1},{1,2},{2,3},{3,4},{4,5},{5,6},{6,7},{7,8},{8,9},{9,10},{10,1... | collective-permute-start | bytes 786440 | tf_op jit(solution)/shard_map/ppermute | solution.py:27
  112.7 83.6 %collective-permute-start.3 = (bf16[128,1024]{1,0:T(8,128)(2,1)}, bf16[128,1024]{1,0:T(8,128)(2,1)}, u32[]{:S(2)}, u32[]{:S(2)}) collective-permute-start(bf16[128,1024]{1,0:T(8,128)(2,1)} %get-tuple-element.17), channel_id=1, source_target_pairs={{1,0},{2,1},{3,2},{4,3},{5,4},{6,5},{7,6},{8,7},{9,8},{10,9},{11,1... | collective-permute-start | bytes 786440 | tf_op jit(solution)/shard_map/ppermute | solution.py:27
Sparse Core Ops, SparseCore 0:
  29.4 49.5 all-gather.3
  115.2 253.2 all-reduce.2
where the time goes:
time: 379 us; the launch traced here: 378 us
  waiting for transfers between devices  221 us (58%)
  blocking collectives  79.3 us (21%)
  other arithmetic  38 us (10%)
  between operations  17.4 us (5%)
  local copies, waits for them, and re-layouts  12.8 us (3%)
  starting transfers between devices  6.4 us (2%)
    psum x1, waiting for transfers between devices, per_device(): sums = lax.psum((wout_part, gain_part, local_loss), ('member', 'grid'))  170 us
    psum x1, blocking collectives, per_device(): sums = lax.psum((wout_part, gain_part, local_loss), ('member', 'grid'))  79.3 us
    all_gather x1, waiting for transfers between devices, per_device(): lax.all_gather(predicted_field[None], 'member', axis=0, tiled=True)  49.7 us
    scatter-add x3, other arithmetic, per_device(): collect.at[neighbours[slot]].add(weight_arrays[slot][:, None] * mixed_grad)  22.9 us
    gather x3, local copies, waits for them, and re-layouts, per_device(): jnp.take(extended, neighbours[slot], axis=0).astype(jnp.float32)  7.64 us
  transfers between devices with their start and end apart: 6, of which 3 were waited for; matrix products, arithmetic and copies ran while one was open for 1% of the time, Pallas kernels for 0%

commit v1 on v0

--- a/solution.py
+++ b/solution.py
@@ -68,7 +68,12 @@
     spread = smooth_abs(pair_distance)
     eps_fair = (1.0 - FAIRNESS) / member_list
     coef_pair = (1.0 - eps_fair) / (member_list * (member_list - 1))
-    every_member_set = lax.all_gather(predicted_field[None], "member", axis=0, tiled=True)
+    every_member_set = jnp.concatenate(
+        lax.all_to_all(
+            jnp.stack([predicted_field[None]] * lax.axis_size("member")), "member", 0, 0
+        ),
+        axis=0,
+    )
     member_difference = predicted_field[None] - every_member_set
     dist = smooth_abs(member_difference)
     pair_total = jnp.sum(dist, axis=0) - SMOOTHING

time: 379 us -> 365 us (0.963)
  waiting for transfers between devices: 221 us -> 194 us
  starting transfers between devices: 6.4 us -> 13.4 us
    all_gather x1 -> x0, waiting for transfers between devices: 49.7 us -> none  [per_device(): lax.all_gather(predicted_field[None], 'member', axis=0, tiled=True)]
    all_to_all x0 -> x1, waiting for transfers between devices: none -> 21.5 us  [per_device(): lax.all_to_all(jnp.stack([predicted_field[None]] * lax.axis_size('member'...]
    all_to_all x0 -> x1, starting transfers between devices: none -> 6.06 us  [per_device(): lax.all_to_all(jnp.stack([predicted_field[None]] * lax.axis_size('member'...]
where the time goes in v1:
time: 365 us; the launch traced here: 364 us
  waiting for transfers between devices  194 us (53%)
  blocking collectives  82.3 us (23%)
  other arithmetic  39 us (11%)
  between operations  17.4 us (5%)
  local copies, waits for them, and re-layouts  16.2 us (4%)
  starting transfers between devices  13.4 us (4%)
    psum x1, waiting for transfers between devices, per_device(): sums = lax.psum((wout_part, gain_part, local_loss), ('member', 'grid'))  171 us
    psum x1, blocking collectives, per_device(): sums = lax.psum((wout_part, gain_part, local_loss), ('member', 'grid'))  82.3 us
    scatter-add x3, other arithmetic, per_device(): collect.at[neighbours[slot]].add(weight_arrays[slot][:, None] * mixed_grad)  22.9 us
    all_to_all x1, waiting for transfers between devices, per_device(): lax.all_to_all(jnp.stack([predicted_field[None]] * lax.axis_size('member'...  21.5 us
    gather x3, local copies, waits for them, and re-layouts, per_device(): jnp.take(extended, neighbours[slot], axis=0).astype(jnp.float32)  8.36 us
  transfers between devices with their start and end apart: 6, of which 3 were waited for; matrix products, arithmetic and copies ran while one was open for 1% of the time, Pallas kernels for 0%

profile of v1, /device:TPU:2, one launch (start us, length us, event | category | flops | bytes accessed | tf_op | source)
XLA Modules:
  0.0 364.5 jit_solution(16021883101506258286)
XLA Ops:
  7.2 0.0 copy-start
  7.2 1.1 fusion.24
  8.3 1.8 collective-permute-start
  10.1 1.3 collective-permute-start.1
  11.4 0.8 fusion.26
  12.2 0.7 reduce_sum.90
  12.9 0.7 broadcast_divide_fusion
  13.7 0.0 collective-permute-done
  13.7 1.5 collective-permute-done.1
  15.2 1.1 maximum_bitcast_fusion
  16.3 2.8 gather_fusion.2
  19.1 2.8 gather_fusion.1
  21.9 2.8 gather_fusion
  24.6 3.0 fusion.21
  27.7 0.0 copy-start.7
  27.7 0.3 multiply_reduce_fusion.2
  28.1 0.0 copy-start.5
  28.1 0.3 copy-done.7
  28.4 0.3 multiply_convert_fusion
  28.7 0.0 copy-done
  28.7 0.3 copy-done.5
  29.0 0.5 fusion.11
  29.5 0.0 copy-start.3
  29.5 0.7 copy-done.3
  30.1 2.0 stack.3
  32.2 0.0 copy-start.8
  32.2 0.0 copy-start.9
  32.2 0.0 copy-start.10
  32.2 6.1 %all-to-all-start = ((f32[8,1,100,512]{3,1,2,0:T(1,128)}), f32[8,1,100,512]{3,1,2,0:T(1,128)}, u32[]{:S(2)}, u32[]{:S(2)}) async-start(f32[8,1,100,512]{3,1,2,0:T(1,128)} %stack.3), calls=%async_computation | async-start | bytes 3276800 | tf_op jit(solution)/shard_map/all_to_all | solution.py:72
  38.2 0.0 all-reduce.3.cloned.1.call-start
  38.2 0.0 copy-done.8
  38.3 21.5 %all-to-all-done = f32[8,1,100,512]{3,1,2,0:T(1,128)} async-done(((f32[8,1,100,512]{3,1,2,0:T(1,128)}), f32[8,1,100,512]{3,1,2,0:T(1,128)}, u32[]{:S(2)}, u32[]{:S(2)}) %all-to-all-start) | async-done | bytes 1638432 | tf_op jit(solution)/shard_map/all_to_all | solution.py:72
  59.8 0.0 copy-start.4
  59.8 0.0 copy-start.6
  59.8 3.3 fusion.10
  63.1 0.0 copy-done.9
  63.1 0.0 copy-done.10
  63.1 0.0 copy-done.4
  63.1 0.0 copy-done.6
  63.1 0.8 fusion.19
  64.0 0.9 multiply_reduce_fusion
  64.9 1.9 subtract_multiply_fusion
  66.8 0.0 copy-start.1
  66.8 7.4 %scatter_custom_fusion = f32[512,1024]{1,0:T(8,128)} fusion(s32[512]{0:T(512)S(1)} %bitcast.55, f32[512,1024]{1,0:T(8,128)} %subtract_multiply_fusion, f32[]{:T(128)} %constant.19.clone.1, f32[512]{0:T(512)S(1)} %bitcast.46), kind=kCustom, calls=%fused_computation.14 | custom fusion | flops 1048576 | bytes 4196356 | tf_op jit(solution)/shard_map/scatter-add | solution.py:99
  74.2 0.0 copy-done.1
  74.2 7.7 %scatter_custom_fusion.1 = f32[512,1024]{1,0:T(8,128)} fusion(f32[512,1024]{1,0:T(8,128)} %scatter_custom_fusion, s32[512]{0:T(512)S(1)} %bitcast.54, f32[512,1024]{1,0:T(8,128)S(1)} %copy-done.1, f32[512]{0:T(512)S(1)} %bitcast.44), kind=kCustom, calls=%fused_computation.12 | custom fusion | flops 1048576 | bytes 4196352 | tf_op jit(solution)/shard_map/scatter-add | solution.py:99
  82.0 7.7 %scatter_custom_fusion.2 = f32[512,1024]{1,0:T(8,128)} fusion(f32[512,1024]{1,0:T(8,128)} %scatter_custom_fusion.1, s32[512]{0:T(512)S(1)} %bitcast.53, f32[512,1024]{1,0:T(8,128)S(1)} %copy-done.1, f32[512]{0:T(512)S(1)} %bitcast.42), kind=kCustom, calls=%fused_computation.10 | custom fusion | flops 1048576 | bytes 4196352 | tf_op jit(solution)/shard_map/scatter-add | solution.py:99
  89.7 1.7 convert.6
  91.5 0.0 copy-start.2
  91.5 0.8 fusion.23
  92.3 3.0 collective-permute-start.2
  95.3 1.3 collective-permute-start.3
  96.6 1.1 fusion.27
  97.7 0.0 all-reduce.3.cloned.1.call-update
  99.0 82.3 %all-reduce = (f32[]{:T(128)}, f32[1024]{0:T(1024)}) all-reduce(f32[]{:T(128)S(6)} %sub.46, f32[1024]{0:T(1024)S(1)} %get-tuple-element.5), channel_id=1, replica_groups=mesh['member'=8,'grid'=32] {'member','grid'}, use_global_device_ids=true, to_apply=%region_6.8 | all-reduce | flops 1025 | bytes 8200 | tf_op jit(solution)/shard_map/psum | solution.py:105
  181.9 0.0 collective-permute-done.2
  181.9 0.0 collective-permute-done.3
  181.9 0.0 copy-done.2
  181.9 2.0 fusion.17
  183.9 170.8 %all-reduce.3.cloned.1.call-done = f32[100,1024]{1,0:T(8,128)} async-done(((f32[100,1024]{1,0:T(8,128)}), f32[100,1024]{1,0:T(8,128)}) %all-reduce.3.cloned.1.call-update) | async-done | bytes 409616 | tf_op jit(solution)/shard_map/psum | solution.py:105
  354.7 1.8 copy.25
  (14 shorter events, 0.1 us)
Async XLA Ops:
  7.2 21.5 %copy-start = (bf16[100,1024]{1,0:T(8,128)(2,1)S(1)}, bf16[100,1024]{1,0:T(8,128)(2,1)}, u32[]{:S(2)}) copy-start(bf16[100,1024]{1,0:T(8,128)(2,1)} %param.20) | copy-start | bytes 614404
  8.3 5.4 %collective-permute-start = (bf16[1,128,1024]{2,1,0:T(8,128)(2,1)S(1)}, bf16[1,128,1024]{2,1,0:T(8,128)(2,1)S(1)}, u32[]{:S(2)}, u32[]{:S(2)}) collective-permute-start(bf16[1,128,1024]{2,1,0:T(8,128)(2,1)S(1)} %get-tuple-element.18), channel_id=1, source_target_pairs={{0,1},{1,2},{2,3},{3,4},{4,5},{5,6},{6,7},{7,8},{8,9},{9,10},{10,1... | collective-permute-start | bytes 786440 | tf_op jit(solution)/shard_map/ppermute | solution.py:18
  10.1 5.1 %collective-permute-start.1 = (bf16[1,128,1024]{2,1,0:T(8,128)(2,1)S(1)}, bf16[1,128,1024]{2,1,0:T(8,128)(2,1)S(1)}, u32[]{:S(2)}, u32[]{:S(2)}) collective-permute-start(bf16[1,128,1024]{2,1,0:T(8,128)(2,1)S(1)} %get-tuple-element.19), channel_id=1, source_target_pairs={{1,0},{2,1},{3,2},{4,3},{5,4},{6,5},{7,6},{8,7},{9,8},{10,9},{11,1... | collective-permute-start | bytes 786440 | tf_op jit(solution)/shard_map/ppermute | solution.py:19
  27.7 0.7 copy-start.7
  28.1 0.9 copy-start.5
  29.5 0.7 copy-start.3
  32.2 6.1 %copy-start.8 = (s32[3,512]{1,0:T(4,128)S(1)}, s32[3,512]{1,0:T(4,128)}, u32[]{:S(2)}) copy-start(s32[3,512]{1,0:T(4,128)} %param.16) | copy-start | bytes 18436
  32.2 30.9 %copy-start.9 = (f32[512]{0:T(512)S(1)}, f32[512]{0:T(512)}, u32[]{:S(2)}) copy-start(f32[512]{0:T(512)} %param.18) | copy-start | bytes 6148
  32.2 31.0 %copy-start.10 = (f32[100]{0:T(128)S(1)}, f32[100]{0:T(128)}, u32[]{:S(2)}) copy-start(f32[100]{0:T(128)} %param.19) | copy-start | bytes 1204
  32.2 27.6 %all-to-all-start = ((f32[8,1,100,512]{3,1,2,0:T(1,128)}), f32[8,1,100,512]{3,1,2,0:T(1,128)}, u32[]{:S(2)}, u32[]{:S(2)}) async-start(f32[8,1,100,512]{3,1,2,0:T(1,128)} %stack.3), calls=%async_computation | async-start | bytes 3276800 | tf_op jit(solution)/shard_map/all_to_all | solution.py:72
  38.2 316.4 %all-reduce.3.cloned.1.call-start = ((), (), s32[]{:S(2)}) async-start(), calls=%async_computation.1 | async-start | bytes 851968 | tf_op jit(solution)/shard_map/psum | solution.py:105
  59.8 3.4 copy-start.4
  59.8 3.4 copy-start.6
  66.8 7.5 %copy-start.1 = (f32[512,1024]{1,0:T(8,128)S(1)}, f32[512,1024]{1,0:T(8,128)}, u32[]{:S(2)}) copy-start(f32[512,1024]{1,0:T(8,128)} %subtract_multiply_fusion) | copy-start | bytes 6291460
  91.5 90.4 %copy-start.2 = (f32[512,1024]{1,0:T(8,128)S(1)}, f32[512,1024]{1,0:T(8,128)}, u32[]{:S(2)}) copy-start(f32[512,1024]{1,0:T(8,128)} %scatter_custom_fusion.2) | copy-start | bytes 6291460
  92.3 89.6 %collective-permute-start.2 = (bf16[128,1024]{1,0:T(8,128)(2,1)}, bf16[128,1024]{1,0:T(8,128)(2,1)}, u32[]{:S(2)}, u32[]{:S(2)}) collective-permute-start(bf16[128,1024]{1,0:T(8,128)(2,1)} %get-tuple-element.16), channel_id=1, source_target_pairs={{0,1},{1,2},{2,3},{3,4},{4,5},{5,6},{6,7},{7,8},{8,9},{9,10},{10,1... | collective-permute-start | bytes 786440 | tf_op jit(solution)/shard_map/ppermute | solution.py:27
  95.3 86.6 %collective-permute-start.3 = (bf16[128,1024]{1,0:T(8,128)(2,1)}, bf16[128,1024]{1,0:T(8,128)(2,1)}, u32[]{:S(2)}, u32[]{:S(2)}) collective-permute-start(bf16[128,1024]{1,0:T(8,128)(2,1)} %get-tuple-element.17), channel_id=1, source_target_pairs={{1,0},{2,1},{3,2},{4,3},{5,4},{6,5},{7,6},{8,7},{9,8},{10,9},{11,1... | collective-permute-start | bytes 786440 | tf_op jit(solution)/shard_map/ppermute | solution.py:27
Sparse Core Ops, SparseCore 0:
  97.8 256.8 all-reduce.2
